TPU v7x, 32 devices: a whole 2x2x4 slice. The times are simulated.
32 devices in a mesh: dom: 8 (over z, y), grp: 4 (over x, core).
Axes of the slice: x: 2, y: 2, z: 4, core: 2. Of those that a mesh axis runs over, the one named last changes fastest.
Arguments:
- residual_in: bfloat16 [256, 32, 625], P(('dom', 'grp')), may hold values from -6 to 6
- block_inverse: bfloat16 [256, 625, 625], P(('dom', 'grp')), may hold values from -0.25 to 0.25
- coupling: bfloat16 [512, 625, 625], P(('dom', 'grp')), may hold values from -0.25 to 0.25
- tile_region: int32 [512, 1], P(('dom', 'grp')), may hold values from 0 to 7; in each aligned block of 16 rows (0 to 15, 16 to 31, ...) at most 2 rows name the same one
- tile_source: int32 [512], P(('dom', 'grp')), may hold values from 0 to 7
- tile_target: int32 [512], P(('dom', 'grp')), may hold values from 0 to 7
- interface_basis: bfloat16 [256, 625, 64], P(('dom', 'grp')), may hold values from -0.25 to 0.25
- reduced_inverse: float32 [8, 64, 64], P('dom'), may hold values from -0.75 to 0.75
Outputs:
- preconditioned: float32 [256, 32, 625], P(('dom', 'grp'))
Inputs may be any that keep to these rules, and one draw needn't show every extreme that they name: `tile_region`: among the 16 tiles of one device, at most 2 name the same region; in every draw some device names some region exactly 2 times.
All inputs are finite; a program needn't handle non-finite values.
Results may differ from a plain program's by a relative error of at most 0.013.
Values may be sent and summed in bfloat16 or wider, within the bound.
A program may use at most 256 MiB of HBM per device.

v0:
```python
import jax
import jax.numpy as jnp
from jax import lax
from jax.sharding import PartitionSpec as P

CAP = 2


def shards(
    residual_in,
    block_inverse,
    coupling,
    tile_region,
    tile_source,
    tile_target,
    interface_basis,
    reduced_inverse,
):
    regions = lax.axis_size("dom")
    slots = regions * CAP
    elements = residual_in.shape[0]
    vectors = residual_in.shape[1]
    width = residual_in.shape[2]
    initial = jnp.einsum(
        "ekb,ebc->ekc", residual_in, block_inverse, preferred_element_type=jnp.float32
    ).astype(jnp.bfloat16)
    destination = tile_region[:, 0]
    onehot = (destination[:, None] == jnp.arange(regions, dtype=jnp.int32)[None, :]).astype(
        jnp.int32
    )
    earlier = jnp.cumsum(onehot, axis=0) - onehot
    tile_rank = jnp.sum(earlier * onehot, axis=1)
    slot_index = destination * CAP + tile_rank
    target_buffer = (
        jnp.full((slots,), -1, jnp.int32).at[slot_index].set(tile_target).reshape(regions, CAP)
    )
    targets = lax.all_to_all(target_buffer, "dom", split_axis=0, concat_axis=0, tiled=True).reshape(
        slots
    )
    sources = initial[tile_source]
    local_products = jnp.einsum(
        "tkb,tbc->tkc", sources, coupling, preferred_element_type=jnp.float32
    )
    product_buffer = (
        jnp.zeros((slots, vectors, width), jnp.float32).at[slot_index].set(local_products)
    )
    products = (
        lax.all_to_all(
            product_buffer.reshape(regions, CAP, vectors, width).astype(jnp.bfloat16),
            "dom",
            split_axis=0,
            concat_axis=0,
            tiled=True,
        )
        .astype(jnp.float32)
        .reshape(slots, vectors, width)
    )
    selector = (targets[None, :] == jnp.arange(elements, dtype=jnp.int32)[:, None]).astype(
        jnp.float32
    )
    coupled = jnp.dot(
        selector,
        products.reshape(slots, vectors * width),
        precision=lax.Precision.HIGHEST,
        preferred_element_type=jnp.float32,
    ).reshape(elements, vectors, width)
    corrected_in = (residual_in.astype(jnp.float32) - coupled).astype(jnp.bfloat16)
    second = jnp.einsum(
        "ekb,ebc->ekc", corrected_in, block_inverse, preferred_element_type=jnp.float32
    )
    second_b = second.astype(jnp.bfloat16)
    partial_reduced = jnp.einsum(
        "ekb,ebm->km", second_b, interface_basis, preferred_element_type=jnp.float32
    )
    reduced = lax.psum(partial_reduced, "grp")
    solved = jnp.dot(
        reduced,
        reduced_inverse[0],
        precision=lax.Precision.HIGHEST,
        preferred_element_type=jnp.float32,
    ).astype(jnp.bfloat16)
    correction = jnp.einsum(
        "km,ebm->ekb", solved, interface_basis, preferred_element_type=jnp.float32
    )
    return second + correction


def solution(mesh):
    return jax.shard_map(
        shards,
        mesh=mesh,
        in_specs=(
            P(("dom", "grp"), None, None),
            P(("dom", "grp"), None, None),
            P(("dom", "grp"), None, None),
            P(("dom", "grp"), None),
            P(("dom", "grp")),
            P(("dom", "grp")),
            P(("dom", "grp"), None, None),
            P("dom", None, None),
        ),
        out_specs=P(("dom", "grp"), None, None),
        check_vma=False,
    )
```

profile of v0, /device:TPU:0, one launch (start us, length us, event | category | flops | bytes accessed | tf_op | source)
XLA Modules:
  0.0 71.7 jit_solution(11191747103379566346)
XLA Ops:
  0.0 0.0 copy-start
  0.0 0.8 %fusion.16 = s32[16,8]{1,0:T(8,128)S(1)} fusion(s32[16]{0:T(128)} %bitcast.35), kind=kLoop, calls=%fused_computation.23 | loop fusion | flops 256 | bytes 576 | tf_op jit(solution)/shard_map/convert_element_type | solution.py:28
  0.8 0.8 %select_reduce_fusion = s32[16]{0:T(128)S(1)} fusion(s32[16,8]{1,0:T(8,128)S(1)} %reduce_window_sum.11, s32[16]{0:T(128)} %bitcast.36), kind=kLoop, calls=%fused_computation.21 | loop fusion | flops 624 | bytes 640 | tf_op jit(solution)/shard_map/reduce_sum | solution.py:32
  1.7 0.7 fusion.20
  2.3 0.8 %scatter_custom_fusion = s32[16]{0:T(128)S(1)} fusion(s32[16]{0:T(128)S(1)} %fusion.20, s32[16]{0:T(128)} %param.13, s32[]{:T(128)} %constant.6.clone.1), kind=kCustom, calls=%fused_computation.32 | custom fusion | bytes 576 | tf_op jit(solution)/shard_map/scatter | solution.py:35
  3.1 0.7 all_to_all.9
  3.8 7.3 %all-to-all-start = ((s32[8,1,2]{2,1,0:T(1,128)}), s32[8,1,2]{2,1,0:T(1,128)S(1)}, u32[]{:S(2)}, u32[]{:S(2)}) async-start(s32[8,1,2]{2,1,0:T(1,128)} %bitcast.3), calls=%async_computation | async-start | bytes 8192 | tf_op jit(solution)/shard_map/all_to_all | solution.py:37
  11.0 0.7 compare_select_fusion
  11.7 5.2 %fusion.7 = bf16[8,32,625]{2,1,0:T(8,128)(2,1)S(1)} fusion(bf16[8,32,625]{2,1,0:T(8,128)(2,1)} %param.8, bf16[8,625,625]{2,0,1:T(8,128)(2,1)} %param.9), kind=kOutput, calls=%fused_computation.12 | convolution fusion | flops 200160000 | bytes 6890000 | tf_op jit(solution)/shard_map/ekb,ebc->ekc/dot_general | solution.py:24
  16.9 0.7 gather_fusion
  17.6 8.7 %fusion = f32[16,32,625]{2,1,0:T(8,128)S(1)} fusion(bf16[16,32,625]{2,1,0:T(8,128)(2,1)S(1)} %gather_fusion, bf16[16,625,625]{2,0,1:T(8,128)(2,1)} %param.10), kind=kOutput, calls=%fused_computation.3 | convolution fusion | flops 400000000 | bytes 14420000 | tf_op jit(solution)/shard_map/tkb,tbc->tkc/dot_general | solution.py:41
  26.3 0.1 broadcast_in_dim.4
  26.4 1.2 %scatter_fusion = f32[16,32,625]{2,1,0:T(8,128)S(1)} fusion(f32[16,32,625]{2,1,0:T(8,128)S(1)} %broadcast_in_dim.4, s32[16]{0:T(128)S(1)} %fusion.20, f32[16,32,625]{2,1,0:T(8,128)S(1)} %fusion), kind=kCustom, calls=%fused_computation.2 | custom fusion | bytes 3840064 | tf_op jit(solution)/shard_map/scatter | solution.py:45
  27.6 0.9 %convert_element_type.29 = bf16[16,32,625]{2,1,0:T(8,128)(2,1)} convert(f32[16,32,625]{2,1,0:T(8,128)S(1)} %scatter_fusion) | non-fusion elementwise | flops 320000 | bytes 1920000 | tf_op jit(solution)/shard_map/convert_element_type | solution.py:49
  28.5 0.0 all-to-all-done
  28.5 6.0 %all-to-all-start.1 = ((bf16[8,2,32,625]{3,2,1,0:T(8,128)(2,1)}), bf16[8,2,32,625]{3,2,1,0:T(8,128)(2,1)S(1)}, u32[]{:S(2)}, u32[]{:S(2)}) async-start(bf16[8,2,32,625]{3,2,1,0:T(8,128)(2,1)} %bitcast.5), calls=%async_computation.1 | async-start | bytes 1310720 | tf_op jit(solution)/shard_map/all_to_all | solution.py:48
  34.5 0.6 broadcast.45
  35.1 0.7 reduce.3
  35.8 0.1 eq.34
  35.9 15.4 %all-to-all-done.1 = bf16[8,2,32,625]{3,2,1,0:T(8,128)(2,1)S(1)} async-done(((bf16[8,2,32,625]{3,2,1,0:T(8,128)(2,1)}), bf16[8,2,32,625]{3,2,1,0:T(8,128)(2,1)S(1)}, u32[]{:S(2)}, u32[]{:S(2)}) %all-to-all-start.1) | async-done | bytes 640032 | tf_op jit(solution)/shard_map/all_to_all | solution.py:48
  51.3 0.7 %reshape_reshape.3 = bf16[16,20000]{1,0:T(8,128)(2,1)S(1)} reshape(bf16[8,2,32,625]{3,2,1,0:T(8,128)(2,1)S(1)} %all-to-all-done.1) | data formatting | bytes 1280000 | tf_op jit(solution)/shard_map/reshape;reshape | solution.py:63
  52.1 0.0 copy-start.1
  52.1 1.6 %dot_general.28 = bf16[32,625,16]{1,0,2:T(8,128)(2,1)S(1)} reshape(bf16[20000,16]{0,1:T(8,128)(2,1)S(1)} %bitcast.34) | data formatting | bytes 1280000 | tf_op jit(solution)/shard_map/dot_general | solution.py:61
  53.6 1.3 %fusion.10 = bf16[8,32,625]{2,0,1:T(8,128)(2,1)S(1)} fusion(bf16[32,625,16]{1,0,2:T(8,128)(2,1)S(1)} %dot_general.28, bf16[8,32,625]{2,1,0:T(8,128)(2,1)} %param.8, s32[16]{0:T(128)S(1)} %eq.34), kind=kOutput, calls=%fused_computation.13 | convolution fusion | flops 5600128 | bytes 1280064 | tf_op jit(solution)/shard_map/dot_general | solution.py:61
  54.9 5.1 %fusion.2 = f32[8,32,625]{2,1,0:T(8,128)S(1)} fusion(bf16[8,625,625]{2,0,1:T(8,128)(2,1)} %param.9, bf16[8,32,625]{2,0,1:T(8,128)(2,1)S(1)} %fusion.10), kind=kOutput, calls=%fused_computation.5 | convolution fusion | flops 200000000 | bytes 7210000 | tf_op jit(solution)/shard_map/ekb,ebc->ekc/dot_general | solution.py:68
  60.0 0.0 copy-done
  60.0 0.3 convolution_bitcast_fusion.1
  60.3 10.1 %psum.7 = f32[32,64]{1,0:T(8,128)S(1)} all-reduce(f32[32,64]{1,0:T(8,128)S(1)} %convolution_bitcast_fusion.1), channel_id=1, replica_groups=mesh['dom'=8,'grp'=4] {'grp'}, use_global_device_ids=true, to_apply=%region_4.5 | all-reduce | flops 2048 | bytes 16384 | tf_op jit(solution)/shard_map/psum | solution.py:75
  70.5 0.0 copy-done.1
  70.5 0.1 fusion.11
  70.6 1.1 %fusion.6 = f32[8,32,625]{2,1,0:T(8,128)} fusion(f32[8,32,625]{2,1,0:T(8,128)S(1)} %fusion.2, bf16[32,64,1]{1,0,2:T(8,128)(2,1)S(1)} %fusion.11, bf16[8,625,64]{1,2,0:T(8,128)(2,1)S(1)} %copy-done), kind=kOutput, calls=%fused_computation.10 | convolution fusion | flops 20640000 | bytes 1924096 | tf_op jit(solution)/shard_map/km,ebm->ekb/dot_general | solution.py:82
  (2 shorter events, 0.0 us)
Async XLA Ops:
  0.0 60.0 %copy-start = (bf16[8,625,64]{1,2,0:T(8,128)(2,1)S(1)}, bf16[8,625,64]{1,2,0:T(8,128)(2,1)}, u32[]{:S(2)}) copy-start(bf16[8,625,64]{1,2,0:T(8,128)(2,1)} %param.14) | copy-start | bytes 1920004
  3.8 24.8 %all-to-all-start = ((s32[8,1,2]{2,1,0:T(1,128)}), s32[8,1,2]{2,1,0:T(1,128)S(1)}, u32[]{:S(2)}, u32[]{:S(2)}) async-start(s32[8,1,2]{2,1,0:T(1,128)} %bitcast.3), calls=%async_computation | async-start | bytes 8192 | tf_op jit(solution)/shard_map/all_to_all | solution.py:37
  28.5 22.8 %all-to-all-start.1 = ((bf16[8,2,32,625]{3,2,1,0:T(8,128)(2,1)}), bf16[8,2,32,625]{3,2,1,0:T(8,128)(2,1)S(1)}, u32[]{:S(2)}, u32[]{:S(2)}) async-start(bf16[8,2,32,625]{3,2,1,0:T(8,128)(2,1)} %bitcast.5), calls=%async_computation.1 | async-start | bytes 1310720 | tf_op jit(solution)/shard_map/all_to_all | solution.py:48
  52.1 18.4 %copy-start.1 = (f32[1,64,64]{2,1,0:T(8,128)S(1)}, f32[1,64,64]{2,1,0:T(8,128)}, u32[]{:S(2)}) copy-start(f32[1,64,64]{2,1,0:T(8,128)} %param.15) | copy-start | bytes 49156
where the time goes:
time: 72.1 us; the launch traced here: 71.7 us
  matrix products  21.8 us (30%)
  waiting for transfers between devices  15.4 us (21%)
  starting transfers between devices  13.3 us (18%)
  blocking collectives  10.1 us (14%)
  local copies, waits for them, and re-layouts  6.4 us (9%)
  other arithmetic  4.61 us (6%)
    all_to_all x1, waiting for transfers between devices, shards(): lax.all_to_all(product_buffer.reshape(regions, CAP, vectors, width).astyp...  15.4 us
    psum x1, blocking collectives, shards(): reduced = lax.psum(partial_reduced, 'grp')  10.1 us
    dot_general x1, matrix products, shards(): jnp.einsum('tkb,tbc->tkc', sources, coupling, preferred_element_type=jnp....  8.7 us
    all_to_all x1, starting transfers between devices, shards(): lax.all_to_all(target_buffer, 'dom', split_axis=0, concat_axis=0, tiled=T...  7.28 us
    all_to_all x1, starting transfers between devices, shards(): lax.all_to_all(product_buffer.reshape(regions, CAP, vectors, width).astyp...  6 us
    dot_general x1, matrix products, shards(): jnp.einsum('ekb,ebc->ekc', residual_in, block_inverse, preferred_element_...  5.17 us
    dot_general x1, matrix products, shards(): jnp.einsum('ekb,ebc->ekc', corrected_in, block_inverse, preferred_element...  5.13 us
    dot_general x1, local copies, waits for them, and re-layouts, shards(): jnp.dot(selector, products.reshape(slots, vectors * width), precision=lax...  1.55 us
  transfers between devices with their start and end apart: 2, of which 1 were waited for; matrix products, arithmetic and copies ran while one was open for 26% of the time, Pallas kernels for 0%

commit v1 on v0

v1 whole, which is shorter than its diff:
```python
import functools

import jax
import jax.numpy as jnp
from jax import lax
from jax.experimental import pallas as pl
from jax.experimental.pallas import tpu as pltpu
from jax.sharding import PartitionSpec as P

CAP = 2
F32 = jnp.float32
BF16 = jnp.bfloat16


def partner(me, offset, count):
    other, bit = 0, 1
    while bit < count:
        other = other + ((me // bit + offset // bit) % 2) * bit
        bit *= 2
    return other


def spread_apply(rows, spread, weights, total, ready):
    height, width = rows.shape
    blocks = weights.shape[1]
    step = spread.shape[0]
    depth = height // blocks
    for start in range(0, width, step):
        size = min(step, width - start)
        wide = jnp.dot(
            rows[:, start : start + size],
            spread[:size, : size * blocks],
            preferred_element_type=F32,
        )
        row = lax.broadcasted_iota(jnp.int32, wide.shape, 0) // depth
        column = lax.broadcasted_iota(jnp.int32, wide.shape, 1) % blocks
        wide = jnp.where(row == column, wide, 0.0).astype(BF16)
        ready(start // step)
        block = weights[start : start + size].reshape(size * blocks, width)
        part = jnp.dot(wide, block, preferred_element_type=F32)
        if start == 0:
            total[...] = part
        else:
            total[...] += part


def kernel(
    regions,
    groups,
    region_ref,
    source_ref,
    target_ref,
    residual_hbm,
    binv_hbm,
    coupling_hbm,
    basis_hbm,
    rinv_hbm,
    out_hbm,
    binv,
    coupling,
    basis,
    basis_t,
    residual,
    rinv,
    initial,
    gathered,
    products,
    corrected,
    spread,
    total,
    acc,
    second,
    send,
    recv,
    meta_send,
    meta_recv,
    red_send,
    red_recv,
    perm,
    meta_smem,
    load_sem,
    binv_sem,
    coupling_sem,
    out_sem,
    send_sem,
    recv_sem,
    meta_send_sem,
    meta_recv_sem,
    meta_local_sem,
    red_send_sem,
    red_recv_sem,
):
    dom, grp = lax.axis_index("dom"), lax.axis_index("grp")
    elements, vectors, width = initial.shape
    tiles = products.shape[0]
    parts, blocks = coupling.shape[0], coupling.shape[2]
    modes = basis_t.shape[1]
    step = spread.shape[0]
    starts = list(range(0, width, step))
    half = regions // 2

    load_residual = pltpu.make_async_copy(residual_hbm, residual, load_sem.at[0])
    load_basis = pltpu.make_async_copy(basis_hbm, basis_t, load_sem.at[1])
    load_rinv = pltpu.make_async_copy(rinv_hbm.at[0], rinv, load_sem.at[2])

    def load_binv(i):
        rows = pl.ds(starts[i], min(step, width - starts[i]))
        return pltpu.make_async_copy(binv_hbm.at[rows], binv.at[rows], binv_sem.at[i])

    def load_coupling(h, i):
        rows = pl.ds(starts[i], min(step, width - starts[i]))
        return pltpu.make_async_copy(
            coupling_hbm.at[rows, h], coupling.at[h, rows], coupling_sem.at[h, i]
        )

    load_residual.start()
    for i in range(len(starts)):
        load_binv(i).start()
    for h in range(parts):
        for i in range(len(starts)):
            load_coupling(h, i).start()
    load_basis.start()
    load_rinv.start()

    barrier = pltpu.get_barrier_semaphore()
    for k in range(1, regions):
        pl.semaphore_signal(barrier, inc=1, device_id=(partner(dom, k, regions), grp))
    for j in range(1, groups):
        pl.semaphore_signal(barrier, inc=1, device_id=(dom, partner(grp, j, groups)))

    row = lax.broadcasted_iota(jnp.int32, spread.shape, 0)
    column = lax.broadcasted_iota(jnp.int32, spread.shape, 1) // blocks
    spread[...] = jnp.where(row == column, 1.0, 0.0).astype(BF16)

    named = [region_ref[t] for t in range(tiles)]
    for k in range(regions):
        place = partner(dom, k, regions)
        first, last = jnp.int32(tiles), jnp.int32(-1)
        for t in range(tiles):
            last = jnp.where(named[t] == place, t, last)
            first = jnp.where(named[tiles - 1 - t] == place, tiles - 1 - t, first)
        has_first = last >= 0
        has_last = last > first
        first = jnp.where(has_first, first, 0)
        last = jnp.where(has_last, last, 0)
        perm[CAP * k] = first
        perm[CAP * k + 1] = last
        aim_first = jnp.where(has_first, target_ref[first], -1)
        aim_last = jnp.where(has_last, target_ref[last], -1)
        meta_send[k, 0:1, :] = jnp.full((1, 128), aim_first, jnp.int32)
        meta_send[k, 1:2, :] = jnp.full((1, 128), aim_last, jnp.int32)

    load_residual.wait()

    def rows_of(e):
        return pl.ds(e * vectors, vectors)

    spread_apply(residual, spread, binv, total, lambda i: load_binv(i).wait())
    for e in range(elements):
        initial[e] = total[rows_of(e)].astype(BF16)

    for t in range(tiles):
        gathered[rows_of(t)] = initial[source_ref[t]]
    for h in range(parts):
        spread_apply(
            gathered.at[pl.ds(h * blocks * vectors, blocks * vectors)],
            spread,
            coupling.at[h],
            total,
            lambda i, h=h: load_coupling(h, i).wait(),
        )
        for i in range(blocks):
            products[h * blocks + i] = total[rows_of(i)].astype(BF16)

    def meta_copy(k):
        return pltpu.make_async_remote_copy(
            src_ref=meta_send.at[k],
            dst_ref=meta_recv.at[k],
            send_sem=meta_send_sem.at[k],
            recv_sem=meta_recv_sem.at[k],
            device_id=(partner(dom, k, regions), grp),
        )

    def product_copy(k, c):
        s = CAP * k + c
        return pltpu.make_async_remote_copy(
            src_ref=send.at[s],
            dst_ref=recv.at[s],
            send_sem=send_sem.at[s],
            recv_sem=recv_sem.at[s],
            device_id=(partner(dom, k, regions), grp),
        )

    pl.semaphore_wait(barrier, regions - 1 + groups - 1)
    for k in range(1, regions):
        meta_copy(k).start()

    def send_products(i, carry):
        k = regions - 1 - i
        for c in range(CAP):
            send[CAP * k + c] = products[perm[CAP * k + c]]
            product_copy(k, c).start()
        return carry

    lax.fori_loop(0, regions - 1, send_products, 0)
    meta_recv[0] = meta_send[0]
    for c in range(CAP):
        recv[c] = products[perm[c]]

    load_basis.wait()
    load_rinv.wait()
    for e in range(elements):
        basis[e] = jnp.swapaxes(basis_t[e].astype(F32), 0, 1).astype(BF16)
        acc[e] = residual[e * vectors : (e + 1) * vectors].astype(F32)
    for k in range(1, regions):
        meta_copy(k).wait()
    meta_local = pltpu.make_async_copy(meta_recv, meta_smem, meta_local_sem.at[0])
    meta_local.start()
    meta_local.wait()

    def weight(k, c, e):
        return jnp.where(meta_smem[k, c, 0] == e, 1.0, 0.0).astype(F32)

    def remaining(k, e, left, right):
        return acc[e] - (weight(k, 0, e) * left + weight(k, 1, e) * right)

    def absorb(k):
        left = recv[CAP * k].astype(F32)
        right = recv[CAP * k + 1].astype(F32)
        for e in range(elements):
            acc[e] = remaining(k, e, left, right)

    def arrive(k):
        for c in range(CAP):
            product_copy(k, c).wait_recv()
        absorb(k)

    def near(i, carry):
        arrive(i + 1)
        return carry

    def far(i, carry):
        arrive(regions - 1 - i)
        return carry

    absorb(0)
    lax.fori_loop(0, half - 1, near, 0)
    lax.fori_loop(0, half - 1, far, 0)
    for c in range(CAP):
        product_copy(half, c).wait_recv()
    left = recv[CAP * half].astype(F32)
    right = recv[CAP * half + 1].astype(F32)
    for e in range(elements):
        corrected[e * vectors : (e + 1) * vectors] = remaining(half, e, left, right).astype(BF16)

    spread_apply(corrected, spread, binv, total, lambda i: None)
    reduced = jnp.zeros((vectors, modes), F32)
    for e in range(elements):
        reduced = reduced + jnp.dot(
            total[rows_of(e)].astype(BF16), basis[e], preferred_element_type=F32
        )
    red_send[...] = reduced

    def red_copy(j):
        return pltpu.make_async_remote_copy(
            src_ref=red_send,
            dst_ref=red_recv.at[j - 1],
            send_sem=red_send_sem.at[j - 1],
            recv_sem=red_recv_sem.at[j - 1],
            device_id=(dom, partner(grp, j, groups)),
        )

    for j in range(1, groups):
        red_copy(j).start()
    for j in range(1, groups):
        red_copy(j).wait()
        reduced = reduced + red_recv[j - 1]
    solved = jnp.dot(
        reduced, rinv[...], precision=lax.Precision.HIGHEST, preferred_element_type=F32
    ).astype(BF16)

    def store(e):
        return pltpu.make_async_copy(second.at[e], out_hbm.at[e], out_sem.at[e])

    for e in range(elements):
        second[e] = total[rows_of(e)] + jnp.dot(solved, basis_t[e], preferred_element_type=F32)
        store(e).start()
    for k in range(1, regions):
        for c in range(CAP):
            product_copy(k, c).wait_send()
    for e in range(elements):
        store(e).wait()


def shards(
    residual_in,
    block_inverse,
    coupling,
    tile_region,
    tile_source,
    tile_target,
    interface_basis,
    reduced_inverse,
):
    regions, groups = lax.axis_size("dom"), lax.axis_size("grp")
    elements, vectors, width = residual_in.shape
    tiles = coupling.shape[0]
    modes = interface_basis.shape[2]
    slots = regions * CAP
    parts = tiles // elements
    step = 128
    chunks = -(-width // step)
    smem = pl.BlockSpec(memory_space=pltpu.SMEM)
    hbm = pl.BlockSpec(memory_space=pl.ANY)
    dma = pltpu.SemaphoreType.DMA
    return pl.pallas_call(
        functools.partial(kernel, regions, groups),
        out_shape=jax.ShapeDtypeStruct((elements, vectors, width), F32),
        in_specs=[smem] * 3 + [hbm] * 5,
        out_specs=hbm,
        scratch_shapes=[
            pltpu.VMEM((width, elements, width), BF16),
            pltpu.VMEM((parts, width, elements, width), BF16),
            pltpu.VMEM((elements, width, modes), BF16),
            pltpu.VMEM((elements, modes, width), BF16),
            pltpu.VMEM((elements * vectors, width), BF16),
            pltpu.VMEM((modes, modes), F32),
            pltpu.VMEM((elements, vectors, width), BF16),
            pltpu.VMEM((tiles * vectors, width), BF16),
            pltpu.VMEM((tiles, vectors, width), BF16),
            pltpu.VMEM((elements * vectors, width), BF16),
            pltpu.VMEM((step, step * elements), BF16),
            pltpu.VMEM((elements * vectors, width), F32),
            pltpu.VMEM((elements, vectors, width), F32),
            pltpu.VMEM((elements, vectors, width), F32),
            pltpu.VMEM((slots, vectors, width), BF16),
            pltpu.VMEM((slots, vectors, width), BF16),
            pltpu.VMEM((regions, 8, 128), jnp.int32),
            pltpu.VMEM((regions, 8, 128), jnp.int32),
            pltpu.VMEM((vectors, modes), F32),
            pltpu.VMEM((groups - 1, vectors, modes), F32),
            pltpu.SMEM((slots,), jnp.int32),
            pltpu.SMEM((regions, 8, 128), jnp.int32),
            dma((3,)),
            dma((chunks,)),
            dma((parts, chunks)),
            dma((elements,)),
            dma((slots,)),
            dma((slots,)),
            dma((regions,)),
            dma((regions,)),
            dma((1,)),
            dma((groups - 1,)),
            dma((groups - 1,)),
        ],
        compiler_params=pltpu.CompilerParams(
            collective_id=0, has_side_effects=True, vmem_limit_bytes=56 * 1024 * 1024
        ),
        cost_estimate=pl.CostEstimate(
            flops=2 * vectors * width * width * (2 * elements + tiles),
            bytes_accessed=2 * width * width * (elements + tiles),
            transcendentals=0,
        ),
    )(
        tile_region[:, 0],
        tile_source,
        tile_target,
        residual_in.reshape(elements * vectors, width),
        jnp.transpose(block_inverse, (1, 0, 2)),
        jnp.transpose(coupling, (1, 0, 2)).reshape(width, parts, elements, width),
        jnp.swapaxes(interface_basis, 1, 2),
        reduced_inverse,
    )


def solution(mesh):
    return jax.shard_map(
        shards,
        mesh=mesh,
        in_specs=(
            P(("dom", "grp"), None, None),
            P(("dom", "grp"), None, None),
            P(("dom", "grp"), None, None),
            P(("dom", "grp"), None),
            P(("dom", "grp")),
            P(("dom", "grp")),
            P(("dom", "grp"), None, None),
            P("dom", None, None),
        ),
        out_specs=P(("dom", "grp"), None, None),
        check_vma=False,
    )
```

time: 72.1 us -> 46.1 us (0.64)
  Pallas kernels: 0 us -> 44 us
  matrix products: 21.8 us -> 0 us
  waiting for transfers between devices: 15.4 us -> 0 us
  starting transfers between devices: 13.3 us -> 0 us
  blocking collectives: 10.1 us -> 0 us
  other arithmetic: 4.61 us -> 0 us
  local copies, waits for them, and re-layouts: 6.4 us -> 1.97 us
    pallas_call x0 -> x1, Pallas kernels: none -> 44 us  [shards(): pl.pallas_call(functools.partial(kernel, regions, groups), out_shape=jax....]
    dot_general x7 -> x0, matrix products: 21.8 us -> none  [the longest x1 8.7 us: shards(): jnp.einsum('tkb,tbc->tkc', sources, coupling, preferred_element_type=jnp....]
    all_to_all x2 -> x0, waiting for transfers between devices: 15.4 us -> none  [the longest x1 15.4 us: shards(): lax.all_to_all(product_buffer.reshape(regions, CAP, vectors, width).astyp...]
    all_to_all x2 -> x0, starting transfers between devices: 13.3 us -> none  [the longest x1 7.28 us: shards(): lax.all_to_all(target_buffer, 'dom', split_axis=0, concat_axis=0, tiled=T...]
    psum x1 -> x0, blocking collectives: 10.1 us -> none  [shards(): reduced = lax.psum(partial_reduced, 'grp')]
    scatter x2 -> x0, local copies, waits for them, and re-layouts: 1.97 us -> none  [the longest x1 1.22 us: shards(): jnp.zeros((slots, vectors, width), jnp.float32).at[slot_index]]
    unnamed x4 -> x1, local copies, waits for them, and re-layouts: 0.01 us -> 1.97 us
    convert_element_type x2 -> x0, other arithmetic: 1.7 us -> none  [the longest x1 0.91 us: shards(): product_buffer.reshape(regions, CAP, vectors, width).astype(jnp.bfloat16)]
  transfers between devices with their start and end apart: 2 -> 0, of which waited for: 1 -> 0; matrix products, arithmetic and copies ran while one was open for 26% -> 0% of each run, Pallas kernels for 0% -> 0%
where the time goes in v1:
time: 46.1 us; the launch traced here: 45.9 us
  Pallas kernels  44 us (95%)
  local copies, waits for them, and re-layouts  1.97 us (4%)
    pallas_call x1, Pallas kernels, shards(): pl.pallas_call(functools.partial(kernel, regions, groups), out_shape=jax....  44 us
    unnamed x1, local copies, waits for them, and re-layouts  1.97 us

profile of v1, /device:TPU:0, one launch (start us, length us, event | category | flops | bytes accessed | tf_op | source)
XLA Modules:
  0.0 45.9 jit_solution(2338539807203369543)
XLA Ops:
  0.0 44.0 %shard_map.82 = f32[8,32,625]{2,1,0:T(8,128)} custom-call(s32[16]{0:T(128)} %bitcast.11, s32[16]{0:T(128)} %source_ref.1, s32[16]{0:T(128)} %target_ref.1, bf16[256,625]{1,0:T(8,128)(2,1)} %bitcast.10, bf16[625,8,625]{2,1,0:T(8,128)(2,1)} %bitcast.8, bf16[625,2,8,625]{3,2,1,0:T(8,128)(2,1)} %bitcast.7, bf16[8,64,625]{2,1,0:T(8,128)(2,1)} %bitcast.9, ...), custom_call_target="tpu_custom_call" | custom-call | flops 800000000 | bytes 18750000 | tf_op jit(solution)/shard_map/pallas_call | solution.py:316
  44.0 2.0 %copy.10 = f32[8,32,625]{2,1,0:T(8,128)} copy(f32[8,32,625]{2,1,0:T(8,128)} %shard_map.82) | data formatting | bytes 1280000

commit v2 on v1

v2 whole, which is shorter than its diff:
```python
import functools

import jax
import jax.numpy as jnp
from jax import lax
from jax.experimental import pallas as pl
from jax.experimental.pallas import tpu as pltpu
from jax.sharding import PartitionSpec as P

CAP = 2
F32 = jnp.float32
BF16 = jnp.bfloat16


def partner(me, offset, count):
    other, bit = 0, 1
    while bit < count:
        other = other + ((me // bit + offset // bit) % 2) * bit
        bit *= 2
    return other


def chunks_of(start, stop, step):
    return [(low, min(low + step, stop)) for low in range(start, stop, step)]


def widen(rows, spread, blocks, depth):
    size = rows.shape[1]
    wide = jnp.dot(rows, spread[:size, : size * blocks], preferred_element_type=F32)
    row = lax.broadcasted_iota(jnp.int32, wide.shape, 0) // depth
    column = lax.broadcasted_iota(jnp.int32, wide.shape, 1) % blocks
    return jnp.where(row == column, wide, 0.0).astype(BF16)


def block_rows(weights, low, high, left, right):
    value = weights[low:high, :, left:right]
    return value.reshape((high - low) * weights.shape[1], right - left)


def kernel(
    regions,
    groups,
    region_ref,
    source_ref,
    target_ref,
    residual_hbm,
    binv_hbm,
    coupling_hbm,
    basis_hbm,
    rinv_hbm,
    second,
    solved,
    binv,
    coupling,
    basis,
    basis_t,
    residual,
    rinv,
    initial,
    gathered,
    wide,
    spread,
    total,
    products,
    corrected,
    send,
    recv,
    meta_send,
    meta_recv,
    red_send,
    red_recv,
    perm,
    meta_smem,
    load_sem,
    binv_sem,
    coupling_sem,
    send_sem,
    recv_sem,
    meta_send_sem,
    meta_recv_sem,
    meta_local_sem,
    red_send_sem,
    red_recv_sem,
):
    dom, grp = lax.axis_index("dom"), lax.axis_index("grp")
    elements, vectors, width = initial.shape
    tiles = products[0].shape[0]
    parts, blocks = coupling.shape[0], coupling.shape[2]
    modes = basis_t.shape[1]
    step = spread.shape[0]
    chunks = chunks_of(0, width, step)
    pieces = chunks_of(0, width, products[0].shape[2])

    load_residual = pltpu.make_async_copy(residual_hbm, residual, load_sem.at[0])
    load_basis = pltpu.make_async_copy(basis_hbm, basis_t, load_sem.at[1])
    load_rinv = pltpu.make_async_copy(rinv_hbm.at[0], rinv, load_sem.at[2])

    def load_binv(i):
        low, high = chunks[i]
        rows = pl.ds(low, high - low)
        return pltpu.make_async_copy(binv_hbm.at[rows], binv.at[rows], binv_sem.at[i])

    def load_coupling(h, i):
        low, high = chunks[i]
        rows = pl.ds(low, high - low)
        return pltpu.make_async_copy(
            coupling_hbm.at[rows, h], coupling.at[h, rows], coupling_sem.at[h, i]
        )

    load_residual.start()
    for i in range(len(chunks)):
        load_binv(i).start()
    for h in range(parts):
        for i in range(len(chunks)):
            load_coupling(h, i).start()
    load_basis.start()
    load_rinv.start()

    barrier = pltpu.get_barrier_semaphore()
    for k in range(1, regions):
        pl.semaphore_signal(barrier, inc=1, device_id=(partner(dom, k, regions), grp))
    for j in range(1, groups):
        pl.semaphore_signal(barrier, inc=1, device_id=(dom, partner(grp, j, groups)))

    row = lax.broadcasted_iota(jnp.int32, spread.shape, 0)
    column = lax.broadcasted_iota(jnp.int32, spread.shape, 1) // blocks
    spread[...] = jnp.where(row == column, 1.0, 0.0).astype(BF16)

    named = [region_ref[t] for t in range(tiles)]
    for k in range(regions):
        place = partner(dom, k, regions)
        first, last = jnp.int32(tiles), jnp.int32(-1)
        for t in range(tiles):
            last = jnp.where(named[t] == place, t, last)
            first = jnp.where(named[tiles - 1 - t] == place, tiles - 1 - t, first)
        has_first = last >= 0
        has_last = last > first
        first = jnp.where(has_first, first, 0)
        last = jnp.where(has_last, last, 0)
        perm[CAP * k] = first
        perm[CAP * k + 1] = last
        aim_first = jnp.where(has_first, target_ref[first], -1)
        aim_last = jnp.where(has_last, target_ref[last], -1)
        meta_send[k, 0:1, :] = jnp.full((1, 128), aim_first, jnp.int32)
        meta_send[k, 1:2, :] = jnp.full((1, 128), aim_last, jnp.int32)

    load_residual.wait()

    def rows_of(e):
        return pl.ds(e * vectors, vectors)

    for i, (low, high) in enumerate(chunks):
        value = widen(residual[:, low:high], spread, blocks, vectors)
        load_binv(i).wait()
        part = jnp.dot(
            value, block_rows(binv, low, high, 0, width), preferred_element_type=F32
        )
        if i == 0:
            total[...] = part
        else:
            total[...] += part
    for e in range(elements):
        initial[e] = total[rows_of(e)].astype(BF16)

    def meta_copy(k):
        return pltpu.make_async_remote_copy(
            src_ref=meta_send.at[k],
            dst_ref=meta_recv.at[k],
            send_sem=meta_send_sem.at[k],
            recv_sem=meta_recv_sem.at[k],
            device_id=(partner(dom, k, regions), grp),
        )

    pl.semaphore_wait(barrier, regions - 1 + groups - 1)
    for k in range(1, regions):
        meta_copy(k).start()
    meta_recv[0] = meta_send[0]

    for t in range(tiles):
        gathered[rows_of(t)] = initial[source_ref[t]]
    for h in range(parts):
        for low, high in chunks:
            wide[h, :, low * blocks : high * blocks] = widen(
                gathered[h * blocks * vectors : (h + 1) * blocks * vectors, low:high],
                spread,
                blocks,
                vectors,
            )

    def product_copy(p, k, c):
        s = CAP * k + c
        return pltpu.make_async_remote_copy(
            src_ref=send[p].at[s],
            dst_ref=recv[p].at[s],
            send_sem=send_sem.at[p, s],
            recv_sem=recv_sem.at[p, s],
            device_id=(partner(dom, k, regions), grp),
        )

    for p, (left, right) in enumerate(pieces):
        for h in range(parts):
            for i, (low, high) in enumerate(chunks):
                if p == 0:
                    load_coupling(h, i).wait()
                part = jnp.dot(
                    wide[h, :, low * blocks : high * blocks],
                    block_rows(coupling.at[h], low, high, left, right),
                    preferred_element_type=F32,
                )
                if i == 0:
                    total[:, left:right] = part
                else:
                    total[:, left:right] += part
            for i in range(blocks):
                products[p][h * blocks + i] = total[rows_of(i), left:right].astype(BF16)

        def send_products(i, carry, p=p):
            k = regions - 1 - i
            for c in range(CAP):
                send[p][CAP * k + c] = products[p][perm[CAP * k + c]]
                product_copy(p, k, c).start()
            return carry

        lax.fori_loop(0, regions - 1, send_products, 0)
        for c in range(CAP):
            recv[p][c] = products[p][perm[c]]

    load_basis.wait()
    load_rinv.wait()
    for e in range(elements):
        basis[e] = jnp.swapaxes(basis_t[e].astype(F32), 0, 1).astype(BF16)
    for k in range(1, regions):
        meta_copy(k).wait()
    meta_local = pltpu.make_async_copy(meta_recv, meta_smem, meta_local_sem.at[0])
    meta_local.start()
    meta_local.wait()

    for p, (left, right) in enumerate(pieces):

        def arrive(k, carry, p=p):
            for c in range(CAP):
                product_copy(p, k, c).wait_recv()
            return carry

        lax.fori_loop(1, regions, arrive, 0)

        def correct(e, carry, p=p):
            value = corrected[p][e].astype(F32)
            for k in range(regions):
                for c in range(CAP):
                    weight = jnp.where(meta_smem[k, c, 0] == e, 1.0, 0.0).astype(F32)
                    value = value - weight * recv[p][CAP * k + c].astype(F32)
            corrected[p][e] = value.astype(BF16)
            return carry

        for e in range(elements):
            corrected[p][e] = residual[rows_of(e), left:right]
        lax.fori_loop(0, elements, correct, 0)
        rows = corrected[p][...].reshape(elements * vectors, right - left)
        for low, high in chunks_of(left, right, step):
            part = jnp.dot(
                widen(rows[:, low - left : high - left], spread, blocks, vectors),
                block_rows(binv, low, high, 0, width),
                preferred_element_type=F32,
            )
            if low == 0:
                total[...] = part
            else:
                total[...] += part

    reduced = jnp.zeros((vectors, modes), F32)
    for e in range(elements):
        value = total[rows_of(e)]
        second[e] = value
        reduced = reduced + jnp.dot(
            value.astype(BF16), basis[e], preferred_element_type=F32
        )
    red_send[...] = reduced

    def red_copy(j):
        return pltpu.make_async_remote_copy(
            src_ref=red_send,
            dst_ref=red_recv.at[j - 1],
            send_sem=red_send_sem.at[j - 1],
            recv_sem=red_recv_sem.at[j - 1],
            device_id=(dom, partner(grp, j, groups)),
        )

    for j in range(1, groups):
        red_copy(j).start()
    for p in range(len(pieces)):
        for k in range(1, regions):
            for c in range(CAP):
                product_copy(p, k, c).wait_send()
    for j in range(1, groups):
        red_copy(j).wait()
        reduced = reduced + red_recv[j - 1]
    solved[...] = jnp.dot(
        reduced, rinv[...], precision=lax.Precision.HIGHEST, preferred_element_type=F32
    ).astype(BF16)


def shards(
    residual_in,
    block_inverse,
    coupling,
    tile_region,
    tile_source,
    tile_target,
    interface_basis,
    reduced_inverse,
):
    regions, groups = lax.axis_size("dom"), lax.axis_size("grp")
    elements, vectors, width = residual_in.shape
    tiles = coupling.shape[0]
    modes = interface_basis.shape[2]
    slots = regions * CAP
    parts = tiles // elements
    step = 128
    chunks = len(chunks_of(0, width, step))
    pieces = [high - low for low, high in chunks_of(0, width, 2 * step)]
    smem = pl.BlockSpec(memory_space=pltpu.SMEM)
    vmem = pl.BlockSpec(memory_space=pltpu.VMEM)
    hbm = pl.BlockSpec(memory_space=pl.ANY)
    dma = pltpu.SemaphoreType.DMA
    second, solved = pl.pallas_call(
        functools.partial(kernel, regions, groups),
        out_shape=(
            jax.ShapeDtypeStruct((elements, vectors, width), F32),
            jax.ShapeDtypeStruct((vectors, modes), BF16),
        ),
        in_specs=[smem] * 3 + [hbm] * 5,
        out_specs=(vmem, vmem),
        scratch_shapes=[
            pltpu.VMEM((width, elements, width), BF16),
            pltpu.VMEM((parts, width, elements, width), BF16),
            pltpu.VMEM((elements, width, modes), BF16),
            pltpu.VMEM((elements, modes, width), BF16),
            pltpu.VMEM((elements * vectors, width), BF16),
            pltpu.VMEM((modes, modes), F32),
            pltpu.VMEM((elements, vectors, width), BF16),
            pltpu.VMEM((tiles * vectors, width), BF16),
            pltpu.VMEM((parts, elements * vectors, width * elements), BF16),
            pltpu.VMEM((step, step * elements), BF16),
            pltpu.VMEM((elements * vectors, width), F32),
            [pltpu.VMEM((tiles, vectors, size), BF16) for size in pieces],
            [pltpu.VMEM((elements, vectors, size), BF16) for size in pieces],
            [pltpu.VMEM((slots, vectors, size), BF16) for size in pieces],
            [pltpu.VMEM((slots, vectors, size), BF16) for size in pieces],
            pltpu.VMEM((regions, 8, 128), jnp.int32),
            pltpu.VMEM((regions, 8, 128), jnp.int32),
            pltpu.VMEM((vectors, modes), F32),
            pltpu.VMEM((groups - 1, vectors, modes), F32),
            pltpu.SMEM((slots,), jnp.int32),
            pltpu.SMEM((regions, 8, 128), jnp.int32),
            dma((3,)),
            dma((chunks,)),
            dma((parts, chunks)),
            dma((len(pieces), slots)),
            dma((len(pieces), slots)),
            dma((regions,)),
            dma((regions,)),
            dma((1,)),
            dma((groups - 1,)),
            dma((groups - 1,)),
        ],
        compiler_params=pltpu.CompilerParams(
            collective_id=0, has_side_effects=True, vmem_limit_bytes=56 * 1024 * 1024
        ),
        cost_estimate=pl.CostEstimate(
            flops=2 * vectors * width * width * (2 * elements + tiles),
            bytes_accessed=2 * width * width * (elements + tiles),
            transcendentals=0,
        ),
    )(
        tile_region[:, 0],
        tile_source,
        tile_target,
        residual_in.reshape(elements * vectors, width),
        jnp.transpose(block_inverse, (1, 0, 2)),
        jnp.transpose(coupling, (1, 0, 2)).reshape(width, parts, elements, width),
        jnp.swapaxes(interface_basis, 1, 2),
        reduced_inverse,
    )
    correction = jnp.einsum("km,ebm->ekb", solved, interface_basis, preferred_element_type=F32)
    return second + correction


def solution(mesh):
    return jax.shard_map(
        shards,
        mesh=mesh,
        in_specs=(
            P(("dom", "grp"), None, None),
            P(("dom", "grp"), None, None),
            P(("dom", "grp"), None, None),
            P(("dom", "grp"), None),
            P(("dom", "grp")),
            P(("dom", "grp")),
            P(("dom", "grp"), None, None),
            P("dom", None, None),
        ),
        out_specs=P(("dom", "grp"), None, None),
        check_vma=False,
    )
```

time: 46.1 us -> 43.3 us (0.939)
  Pallas kernels: 44 us -> 40.9 us
  matrix products: 0 us -> 2.18 us
  local copies, waits for them, and re-layouts: 1.97 us -> 0.01 us
    pallas_call x1, Pallas kernels: 44 us -> 40.9 us  [shards(): pl.pallas_call(functools.partial(kernel, regions, groups), out_shape=(jax...]
    dot_general x0 -> x1, matrix products: none -> 2.18 us  [shards(): jnp.einsum('km,ebm->ekb', solved, interface_basis, preferred_element_type...]
    unnamed x1 -> x2, local copies, waits for them, and re-layouts: 1.97 us -> 0.01 us
where the time goes in v2:
time: 43.3 us; the launch traced here: 43 us
  Pallas kernels  40.9 us (94%)
  matrix products  2.18 us (5%)
    pallas_call x1, Pallas kernels, shards(): pl.pallas_call(functools.partial(kernel, regions, groups), out_shape=(jax...  40.9 us
    dot_general x1, matrix products, shards(): jnp.einsum('km,ebm->ekb', solved, interface_basis, preferred_element_type...  2.18 us

profile of v2, /device:TPU:0, one launch (start us, length us, event | category | flops | bytes accessed | tf_op | source)
XLA Modules:
  0.0 43.0 jit_solution(6520113999603235710)
XLA Ops:
  0.0 0.0 copy-start
  0.0 40.9 %shard_map.82 = (f32[8,32,625]{2,1,0:T(8,128)}, bf16[32,64]{1,0:T(8,128)(2,1)}) custom-call(s32[16]{0:T(128)} %bitcast.19, s32[16]{0:T(128)} %source_ref.1, s32[16]{0:T(128)} %target_ref.1, bf16[256,625]{1,0:T(8,128)(2,1)} %bitcast.18, bf16[625,8,625]{2,1,0:T(8,128)(2,1)} %bitcast.16, bf16[625,2,8,625]{3,2,1,0:T(8,128)(2,1)} %bitcast.15, ...), custom_call_target="tpu_custom_call" | custom-call | flops 800000000 | bytes 18750000 | tf_op jit(solution)/shard_map/pallas_call | solution.py:326
  40.9 0.0 copy-done
  40.9 2.2 %fusion = f32[8,32,625]{2,1,0:T(8,128)} fusion(f32[8,32,625]{2,1,0:T(8,128)} %get-tuple-element.7, bf16[8,625,64]{1,2,0:T(8,128)(2,1)S(1)} %copy-done, bf16[32,64]{1,0:T(8,128)(2,1)} %get-tuple-element.8), kind=kOutput, calls=%fused_computation.1 | convolution fusion | flops 20640000 | bytes 1924096 | tf_op jit(solution)/shard_map/km,ebm->ekb/dot_general | solution.py:385
Async XLA Ops:
  0.0 40.9 %copy-start = (bf16[8,625,64]{1,2,0:T(8,128)(2,1)S(1)}, bf16[8,625,64]{1,2,0:T(8,128)(2,1)}, u32[]{:S(2)}) copy-start(bf16[8,625,64]{1,2,0:T(8,128)(2,1)} %param.14) | copy-start | bytes 1920004
